TPU v7x, 32 devices: a whole 2x2x4 slice. The times are simulated.
32 devices in a mesh: gx: 4 (over y, core), gy: 4 (over z), gz: 2 (over x).
Axes of the slice: x: 2, y: 2, z: 4, core: 2. Of those that a mesh axis runs over, the one named last changes fastest.
Arguments:
- positions: float32 [3, 4096], P(None, ('gx', 'gy', 'gz')), as said below
- attributes: float32 [128, 4096], P(None, ('gx', 'gy', 'gz')), may hold values from -6 to 6
- species: int32 [4096], P(('gx', 'gy', 'gz')), may hold values from 0 to 3
- occupied: int32 [4096], P(('gx', 'gy', 'gz')), may hold values from 0 to 1
- neighbours: int32 [32, 4096], P(None, ('gx', 'gy', 'gz')), may hold values from 0 to 977
- pair_flags: int32 [32, 4096], P(None, ('gx', 'gy', 'gz')), may hold values from 0 to 1, as said below
- site_slots: int32 [4096], P(('gx', 'gy', 'gz')), may hold values from 0 to 127, as said below
- radial_weight: float32 [8, 64], replicated, may hold values from -2 to 2
- node_weight: float32 [128, 128], replicated, may hold values from -0.5 to 0.5
- mix_weight: float32 [64, 128], replicated, may hold values from -0.75 to 0.75
- latent_in: float32 [256, 128], replicated, may hold values from -0.375 to 0.375
- latent_out: float32 [128, 64], replicated, may hold values from -0.5 to 0.5
- readout: float32 [64], replicated, may hold values from -0.75 to 0.75
- species_scale: float32 [4], replicated, may hold values from 0.5 to 1.5
- species_shift: float32 [4], replicated, may hold values from -3 to 3
Outputs:
- atom_energy: float32 [4096], P(('gx', 'gy', 'gz'))
- forces: float32 [3, 4096], P(None, ('gx', 'gy', 'gz'))
Inputs may be any that keep to these rules, and one draw needn't show every extreme that they name: `positions`: atoms sit on a jittered lattice of 8 x 8 x 2 sites a brick, spacing 1.5 angstrom; every coordinate lies inside its brick. `pair_flags`: A flag is 1 exactly where the centre and the named atom are both occupied. `site_slots`: within each brick every slot appears once, in an order drawn for each brick.
All inputs are finite; a program needn't handle non-finite values.
Results may differ from a plain program's by a relative error of at most 0.0003.
Values sent between devices are 32-bit elements; how exact they have to be, the bound alone decides.
A program may use at most 64 MiB of HBM per device.

v0:
```python
import functools
import math

import jax
import jax.numpy as jnp
import numpy as np
from jax import lax
from jax.experimental import pallas as pl
from jax.experimental.pallas import tpu as pltpu
from jax.sharding import PartitionSpec as P

LXY = 8
LZ = 2
SITES = LXY * LXY * LZ
SPACING = 1.5
CUTOFF = 4.0
PRECISE = lax.Precision.HIGHEST
R3 = math.sqrt(3.0)
R5 = math.sqrt(5.0)
R15 = math.sqrt(15.0)
AXES = ("gx", "gy", "gz")
F32 = jnp.float32
BF16 = jnp.bfloat16
NT = (((1,), (1,)), ((), ()))
VMEM = pl.BlockSpec(memory_space=pltpu.VMEM)
SMEM = pl.BlockSpec(memory_space=pltpu.SMEM)


def offsets():
    span = range(-2, 3)
    return [
        (dx, dy, dz)
        for dx in span
        for dy in span
        for dz in span
        if 0 < dx * dx + dy * dy + dz * dz <= 4
    ]


def flat(x, y, z):
    return (x * LXY + y) * LZ + z


def lattice_plan(z_bricks):
    z_sides = [1] if z_bricks == 2 else [1, -1]
    groups = {}
    cursor = [SITES]

    def near(side, deep):
        if side == 0:
            return range(LXY)
        if side > 0:
            return range(0, 2 if deep else 1)
        return range(LXY - (2 if deep else 1), LXY)

    def add(o):
        lone = sum(c != 0 for c in o) == 1
        sites = [flat(x, y, z) for x in near(o[0], lone) for y in near(o[1], lone) for z in range(LZ)]
        groups[o] = (cursor[0], sites)
        cursor[0] += -(-len(sites) // 8) * 8

    for o in [(1, 0, 0), (-1, 0, 0), (0, 1, 0), (0, -1, 0)]:
        add(o)
    for oz in z_sides:
        add((0, 0, oz))
    for ox in (1, -1):
        for oy in (1, -1):
            add((ox, oy, 0))
    for oz in z_sides:
        for side in (1, -1):
            add((side, 0, oz))
            add((0, side, oz))
        for ox in (1, -1):
            for oy in (1, -1):
                add((ox, oy, oz))
    rows = -(-cursor[0] // 256) * 256
    select = np.zeros((rows, SITES), np.float32)
    for start, sites in groups.values():
        for n, site in enumerate(sites):
            select[start + n, site] = 1.0
    ds = offsets()
    hot = np.zeros((len(ds), rows, SITES), np.float32)
    shift = np.zeros((3, len(ds), SITES), np.float32)
    edge = (LXY * SPACING, LXY * SPACING, LZ * SPACING)
    for k, d in enumerate(ds):
        for x in range(LXY):
            for y in range(LXY):
                for z in range(LZ):
                    t = (x + d[0], y + d[1], z + d[2])
                    o = (t[0] // LXY, t[1] // LXY, t[2] // LZ)
                    inside = flat(t[0] % LXY, t[1] % LXY, t[2] % LZ)
                    s = flat(x, y, z)
                    for c in range(3):
                        shift[c, k, s] = o[c] * edge[c]
                    if o == (0, 0, 0):
                        g = inside
                    else:
                        key = (o[0], o[1], abs(o[2])) if z_bricks == 2 else o
                        start, sites = groups[key]
                        g = start + sites.index(inside)
                    hot[k, g, s] = 1.0
    count = len(ds) // 2
    hot = np.concatenate([hot[0::2], hot[1::2]], axis=2)
    assert hot.shape == (count, rows, 2 * SITES)
    return groups, select, hot, shift


def device_at(o, sizes):
    return tuple(
        lax.rem(lax.axis_index(a) + (c + n), n) if c else lax.axis_index(a)
        for a, c, n in zip(AXES, o, sizes)
    )


def greet(groups, sizes):
    barrier = pltpu.get_barrier_semaphore()
    for o in groups:
        pl.semaphore_signal(
            barrier, inc=1, device_id=device_at(o, sizes), device_id_type=pl.DeviceIdType.MESH
        )
    return barrier


def dot(a, b):
    return jnp.dot(a, b, preferred_element_type=F32)


def exact(a, b):
    return jnp.dot(a, b, precision=PRECISE, preferred_element_type=F32)


def halves(x):
    high = x.astype(BF16)
    return high, (x - high.astype(F32)).astype(BF16)


def stack_rhs(x):
    high, low = halves(x)
    return jnp.concatenate([high, low, high], axis=0)


def stack_lhs(w):
    high = w.astype(BF16).astype(F32)
    return jnp.concatenate([high, high, w - high], axis=1).astype(BF16)


def slot_site(row):
    slot = lax.broadcasted_iota(jnp.int32, (SITES, SITES), 0)
    return jnp.where(slot == row, 1.0, 0.0).astype(F32)


def ghosts_kernel(
    groups, sizes, rows, scale_ref, shift_ref, pos_ref, attr_ref, species_ref, occ_ref, slots_ref,
    node_ref, select_ref, own_ref, table_ref, send_buf, recv_buf, send_sem, recv_sem,
):
    used = max(start + -(-len(sites) // 8) * 8 for start, sites in groups.values())
    if used < rows:
        recv_buf[used - SITES :, :] = jnp.zeros((rows - used, SITES), F32)
    barrier = greet(groups, sizes)
    terms = exact(node_ref[...].T, attr_ref[...])
    occ = occ_ref[...].astype(F32)
    species = species_ref[...]
    scale = jnp.zeros_like(occ)
    shift = jnp.zeros_like(occ)
    for n in range(scale_ref.shape[0]):
        scale = jnp.where(species == n, scale_ref[n], scale)
        shift = jnp.where(species == n, shift_ref[n], shift)
    extra = jnp.concatenate(
        [pos_ref[...], occ, occ * scale, occ * shift, jnp.zeros((2, SITES), F32)], axis=0
    )
    data = jnp.concatenate([terms, extra], axis=0)
    data = exact(data, slot_site(slots_ref[...]))
    ch = terms.shape[0] // 2
    own_ref[...] = data
    sent = jnp.concatenate([data[ch:], jnp.zeros((SITES - ch - 8, SITES), F32)], axis=0)
    wide = exact(select_ref[...], sent.T)
    send_buf[...] = wide
    pl.semaphore_wait(barrier, len(groups))
    copies = []
    for n, (o, (start, sites)) in enumerate(groups.items()):
        back = tuple(-c for c in o)
        part = pl.ds(start - SITES, -(-len(sites) // 8) * 8)
        copies.append(
            pltpu.make_async_remote_copy(
                src_ref=send_buf.at[part],
                dst_ref=recv_buf.at[part],
                send_sem=send_sem.at[n],
                recv_sem=recv_sem.at[n],
                device_id=device_at(back, sizes),
                device_id_type=pl.DeviceIdType.MESH,
            )
        )
    for copy in copies:
        copy.start()
    for copy in copies:
        copy.wait()

    for t in range(rows // SITES):
        if t == 0:
            near, q = data[ch : 2 * ch], data[2 * ch :]
        else:
            block = recv_buf[(t - 1) * SITES : t * SITES, :].T
            near, q = block[:ch], block[ch : ch + 8]
        near_high = near.astype(BF16).astype(F32)
        q1 = q.astype(BF16).astype(F32)
        q2 = (q - q1).astype(BF16).astype(F32)
        table_ref[:, t * SITES : (t + 1) * SITES] = jnp.concatenate(
            [near_high, near - near_high, q1, q2, q - q1 - q2, jnp.zeros_like(q)], axis=0
        ).astype(BF16)


def sigmoid(v):
    return 1.0 / (1.0 + jnp.exp(-v))


def model_kernel(
    slots, ch, own_ref, table_ref, hot_ref, shift_ref, radial_ref, mix_ref, in_ref, out_w_ref,
    readout_ref, result_ref, near_s, q_s, basis_s, y_s, env_s, first_s, sig_s, gain_s, raw_s, s_s,
    ds_s, dt_s, dfirst_s, dgain_s, scal_s, dbasis_s, dy_s, g_s, lin_s, linb_s,
):
    pairs = slots // 2
    inv_root = 1.0 / math.sqrt(slots)
    table = table_ref[...]

    def fetch(p, carry):
        got = dot(table, hot_ref[p])
        for j in range(2):
            k = 2 * p + j
            part = got[:, j * SITES : (j + 1) * SITES]
            near_s[k] = part[:ch] + part[ch : 2 * ch]
            q = 2 * ch
            q_s[k] = part[q : q + 8] + part[q + 8 : q + 16] + part[q + 16 : q + 24]
        return carry

    lax.fori_loop(0, pairs, fetch, 0)

    extra = own_ref[2 * ch : 2 * ch + 8]
    ebar = extra[4:5]
    rx = (q_s[:, 0, :] + shift_ref[0]) - extra[0:1]
    ry = (q_s[:, 1, :] + shift_ref[1]) - extra[1:2]
    rz = (q_s[:, 2, :] + shift_ref[2]) - extra[2:3]
    flag = q_s[:, 3, :] * extra[3:4]
    d = jnp.sqrt(rx * rx + ry * ry + rz * rz)
    inv = 1.0 / d
    ux, uy, uz = rx * inv, ry * inv, rz * inv
    y_s[:, 0, :] = jnp.ones_like(ux)
    y_s[:, 1, :] = R3 * ux
    y_s[:, 2, :] = R3 * uy
    y_s[:, 3, :] = R3 * uz
    y_s[:, 4, :] = R15 * ux * uy
    y_s[:, 5, :] = R15 * uy * uz
    y_s[:, 6, :] = 0.5 * R5 * (3.0 * uz * uz - 1.0)
    y_s[:, 7, :] = R15 * ux * uz
    y_s[:, 8, :] = 0.5 * R15 * (ux * ux - uy * uy)
    scaled = d * (1.0 / CUTOFF)
    base = 1.0 - scaled * scaled
    env_s[...] = base * base * flag
    denv_dd = base * scaled * flag * (-4.0 / CUTOFF)
    angle = d * (math.pi / CUTOFF)
    sines = [jnp.sin(angle)]
    cosines = [jnp.cos(angle)]
    for n in range(1, radial_ref.shape[0]):
        sines.append(sines[0] * cosines[-1] + cosines[0] * sines[-1])
        cosines.append(cosines[0] * cosines[-1] - sines[0] * sines[n - 1])
    for n in range(radial_ref.shape[0]):
        basis_s[:, n, :] = sines[n] * inv

    centre = own_ref[:ch]
    radial_t = radial_ref[...].T
    mix3_t = stack_lhs(mix_ref[...].T)

    def first(p, carry):
        basis = jnp.concatenate([basis_s[2 * p], basis_s[2 * p + 1]], axis=1)
        radial = exact(radial_t, basis)
        total = []
        for j in range(2):
            k = 2 * p + j
            v = radial[:, j * SITES : (j + 1) * SITES] + centre + near_s[k]
            sig = sigmoid(v)
            act = v * sig
            first_s[k] = act
            sig_s[k] = sig * (1.0 + v * (1.0 - sig))
            total.append(act)
        mixture = dot(mix3_t, stack_rhs(jnp.concatenate(total, axis=1)))
        for j in range(2):
            k = 2 * p + j
            part = mixture[:, j * SITES : (j + 1) * SITES]
            gain_s[k] = part[:ch]
            raw_s[k] = part[ch:]
        return carry

    lax.fori_loop(0, pairs, first, 0)

    step = 16
    for c in range(0, ch, step):

        def gather_s(k, acc):
            w = raw_s[k, c : c + step, :] * env_s[pl.ds(k, 1), :]
            return tuple(a + w * (y_s[k, m : m + 1, :]) if m else a + w for m, a in enumerate(acc))

        acc = lax.fori_loop(
            0, slots, gather_s, tuple(jnp.zeros((step, SITES), F32) for _ in range(9)), unroll=4
        )
        for m in range(9):
            s_s[m, c : c + step, :] = acc[m] * inv_root

    lin_s[...] = stack_lhs(in_ref[...].T)
    linb_s[...] = stack_lhs(in_ref[...])
    readout_row = readout_ref[...]
    v_col = jnp.sum(out_w_ref[...] * readout_row, axis=1, keepdims=True)
    same = lax.broadcasted_iota(jnp.int32, (ch, ch), 0) == lax.broadcasted_iota(jnp.int32, (ch, ch), 1)
    r_col = jnp.sum(jnp.where(same, readout_row, 0.0), axis=1, keepdims=True)

    def middle(p, energy):
        feats, gains, t1s, t2s, envs = [], [], [], [], []
        for j in range(2):
            k = 2 * p + j
            y = [y_s[k, m : m + 1, :] for m in range(9)]
            t1 = y[1] * s_s[1]
            for m in (2, 3):
                t1 = t1 + y[m] * s_s[m]
            t2 = y[4] * s_s[4]
            for m in (5, 6, 7, 8):
                t2 = t2 + y[m] * s_s[m]
            gain = gain_s[k]
            feats.append(jnp.concatenate([first_s[k], gain * s_s[0], gain * t1, gain * t2], axis=0))
            gains.append(gain)
            t1s.append(t1)
            t2s.append(t2)
            envs.append(env_s[pl.ds(k, 1), :])
        hidden = dot(lin_s[...], stack_rhs(jnp.concatenate(feats, axis=1)))
        sig = sigmoid(hidden)
        act = hidden * sig
        slope = sig * (1.0 + hidden * (1.0 - sig))
        weight = jnp.concatenate([e * ebar for e in envs], axis=1)
        dhidden = slope * (v_col * weight)
        dfeat = dot(linb_s[...], stack_rhs(dhidden))
        ract = jnp.sum(v_col * act, axis=0, keepdims=True)
        for j in range(2):
            k = 2 * p + j
            lanes = slice(j * SITES, (j + 1) * SITES)
            raw = ract[:, lanes] + jnp.sum(r_col * feats[j][:ch], axis=0, keepdims=True)
            scal_s[pl.ds(k, 1), :] = raw
            energy = energy + raw * envs[j]
            df = dfeat[:, lanes]
            d0, d1, d2 = df[ch : 2 * ch], df[2 * ch : 3 * ch], df[3 * ch :]
            dfirst_s[k] = df[:ch] + r_col * weight[:, lanes]
            dgain_s[k] = d0 * s_s[0] + d1 * t1s[j] + d2 * t2s[j]
            dt_s[k] = jnp.concatenate([gains[j] * d0, gains[j] * d1, gains[j] * d2], axis=0)
        return energy

    energy = lax.fori_loop(0, pairs, middle, jnp.zeros((1, SITES), F32))

    for c in range(0, ch, step):

        def gather_ds(k, acc):
            t = [dt_s[k, l * ch + c : l * ch + c + step, :] for l in range(3)]
            out = [acc[0] + t[0]]
            for m in range(1, 9):
                out.append(acc[m] + t[1 if m < 4 else 2] * y_s[k, m : m + 1, :])
            return tuple(out)

        acc = lax.fori_loop(
            0, slots, gather_ds, tuple(jnp.zeros((step, SITES), F32) for _ in range(9)), unroll=4
        )
        for m in range(9):
            ds_s[m, c : c + step, :] = acc[m] * inv_root

    mix3 = stack_lhs(mix_ref[...])
    radial3 = stack_lhs(jnp.concatenate([radial_ref[...], jnp.zeros((8, ch), F32)], axis=0))

    def last(p, carry):
        dmix = []
        for j in range(2):
            k = 2 * p + j
            env = env_s[pl.ds(k, 1), :]
            raw = raw_s[k]
            w = raw * env
            t1 = dt_s[k, ch : 2 * ch, :]
            t2 = dt_s[k, 2 * ch :, :]
            dw = ds_s[0]
            for m in range(1, 9):
                dsm = ds_s[m]
                dw = dw + y_s[k, m : m + 1, :] * dsm
                t = t1 if m < 4 else t2
                dy_s[k, m : m + 1, :] = jnp.sum(t * s_s[m] + w * dsm, axis=0, keepdims=True)
            scal_s[pl.ds(k, 1), :] = scal_s[pl.ds(k, 1), :] * ebar + jnp.sum(
                raw * dw, axis=0, keepdims=True
            )
            dmix.append(jnp.concatenate([dgain_s[k], dw * env], axis=0))
        dfirst = dot(mix3, stack_rhs(jnp.concatenate(dmix, axis=1)))
        dsum = []
        for j in range(2):
            k = 2 * p + j
            dsum.append((dfirst[:, j * SITES : (j + 1) * SITES] + dfirst_s[k]) * sig_s[k])
        dbasis = dot(radial3, stack_rhs(jnp.concatenate(dsum, axis=1)))
        for j in range(2):
            dbasis_s[2 * p + j] = dbasis[:8, j * SITES : (j + 1) * SITES]
        return carry

    lax.fori_loop(0, pairs, last, 0)

    dd = scal_s[...] * denv_dd
    for n in range(radial_ref.shape[0]):
        rate = (n + 1) * math.pi / CUTOFF
        dd = dd + dbasis_s[:, n, :] * ((rate * cosines[n] - sines[n] * inv) * inv)
    y1, y2, y3, y4, y5, y6, y7, y8 = [dy_s[:, m, :] for m in range(1, 9)]
    dux = R3 * y1 + R15 * (uy * y4 + uz * y7 + ux * y8)
    duy = R3 * y2 + R15 * (ux * y4 + uz * y5 - uy * y8)
    duz = R3 * y3 + R15 * (uy * y5 + ux * y7) + 3.0 * R5 * uz * y6
    along = dd - (ux * dux + uy * duy + uz * duz) * inv
    zero = jnp.zeros_like(d)
    own = []
    for n, (u, du) in enumerate(((ux, dux), (uy, duy), (uz, duz))):
        g = u * along + du * inv
        own.append(jnp.sum(g, axis=0, keepdims=True))
        high = g.astype(BF16).astype(F32)
        g_s[:, n, :] = high
        g_s[:, 8 + n, :] = g - high
    for n in range(3, 8):
        g_s[:, n, :] = zero
        g_s[:, 8 + n, :] = zero

    def spread(p, acc):
        g = jnp.concatenate([g_s[2 * p], g_s[2 * p + 1]], axis=1).astype(BF16)
        return acc + lax.dot_general(g, hot_ref[p], NT, preferred_element_type=F32)

    rows = table_ref.shape[1]
    acc = lax.fori_loop(0, pairs, spread, jnp.zeros((16, rows), F32))
    acc = -(acc[:8] + acc[8:])
    own.append(ebar * energy + extra[5:6])
    own.append(jnp.zeros((4, SITES), F32))
    result_ref[0] = acc[:, :SITES] + jnp.concatenate(own, axis=0)
    for t in range(1, rows // SITES):
        result_ref[t] = acc[:, t * SITES : (t + 1) * SITES]


def return_kernel(
    groups, sizes, part_ref, slots_ref, select_ref, out_ref, recv_buf, send_sem, recv_sem
):
    barrier = greet(groups, sizes)
    pl.semaphore_wait(barrier, len(groups))
    copies = []
    for n, (o, (start, _)) in enumerate(groups.items()):
        copies.append(
            pltpu.make_async_remote_copy(
                src_ref=part_ref.at[start // SITES],
                dst_ref=recv_buf.at[n],
                send_sem=send_sem.at[n],
                recv_sem=recv_sem.at[n],
                device_id=device_at(o, sizes),
                device_id_type=pl.DeviceIdType.MESH,
            )
        )
    for copy in copies:
        copy.start()
    for copy in copies:
        copy.wait()
    lane = lax.broadcasted_iota(jnp.int32, (8, SITES), 1)
    total = part_ref[0]
    merged = [jnp.zeros((8, SITES), F32) for _ in range(part_ref.shape[0])]
    for n, (start, sites) in enumerate(groups.values()):
        t, low = start // SITES, start % SITES
        live = (lane >= low) & (lane < low + len(sites))
        merged[t] = merged[t] + jnp.where(live, recv_buf[n], 0.0)
    total = total + exact(
        jnp.concatenate(merged[1:], axis=1), select_ref[...]
    )
    out_ref[...] = lax.dot_general(
        total, slot_site(slots_ref[...]), NT, precision=PRECISE, preferred_element_type=F32
    )


def shards(
    sizes,
    positions,
    attributes,
    species,
    occupied,
    neighbours,
    pair_flags,
    site_slots,
    radial_weight,
    node_weight,
    mix_weight,
    latent_in,
    latent_out,
    readout,
    species_scale,
    species_shift,
):
    groups, select, hot, shift = lattice_plan(sizes[2])
    rows = hot.shape[1]
    slots = shift.shape[1]
    ch = mix_weight.shape[0]
    hid = latent_in.shape[1]
    count = len(groups)
    select = jnp.asarray(select[SITES:])
    hot = jnp.asarray(hot, dtype=BF16)
    site_row = site_slots.reshape(1, SITES)
    own, table = pl.pallas_call(
        functools.partial(ghosts_kernel, groups, sizes, rows),
        out_shape=(
            jax.ShapeDtypeStruct((2 * ch + 8, SITES), F32),
            jax.ShapeDtypeStruct((2 * ch + 32, rows), BF16),
        ),
        in_specs=[SMEM] * 2 + [VMEM] * 7,
        out_specs=(VMEM, VMEM),
        scratch_shapes=[
            pltpu.VMEM((rows - SITES, SITES), F32),
            pltpu.VMEM((rows - SITES, SITES), F32),
            pltpu.SemaphoreType.DMA((count,)),
            pltpu.SemaphoreType.DMA((count,)),
        ],
        compiler_params=pltpu.CompilerParams(
            collective_id=0, has_side_effects=True, vmem_limit_bytes=16 * 2**20
        ),
        name="ghosts",
    )(
        species_scale,
        species_shift,
        positions,
        attributes,
        species.reshape(1, SITES),
        occupied.reshape(1, SITES),
        site_row,
        node_weight,
        select,
    )
    per_slot = lambda *dims: pltpu.VMEM((slots,) + dims + (SITES,), F32)
    parts = pl.pallas_call(
        functools.partial(model_kernel, slots, ch),
        out_shape=jax.ShapeDtypeStruct((rows // SITES, 8, SITES), F32),
        in_specs=[VMEM] * 9,
        out_specs=VMEM,
        scratch_shapes=[
            per_slot(ch),
            per_slot(8),
            per_slot(8),
            per_slot(16),
            per_slot(),
            per_slot(ch),
            per_slot(ch),
            per_slot(ch),
            per_slot(ch),
            pltpu.VMEM((9, ch, SITES), F32),
            pltpu.VMEM((9, ch, SITES), F32),
            per_slot(3 * ch),
            per_slot(ch),
            per_slot(ch),
            per_slot(),
            per_slot(8),
            per_slot(16),
            per_slot(16),
            pltpu.VMEM((hid, 12 * ch), BF16),
            pltpu.VMEM((4 * ch, 3 * hid), BF16),
        ],
        compiler_params=pltpu.CompilerParams(vmem_limit_bytes=40 * 2**20),
        name="model",
    )(
        own,
        table,
        hot,
        jnp.asarray(shift),
        radial_weight,
        mix_weight,
        latent_in,
        latent_out,
        readout.reshape(1, ch),
    )
    out = pl.pallas_call(
        functools.partial(return_kernel, groups, sizes),
        out_shape=jax.ShapeDtypeStruct((8, SITES), F32),
        in_specs=[VMEM] * 3,
        out_specs=VMEM,
        scratch_shapes=[
            pltpu.VMEM((count, 8, SITES), F32),
            pltpu.SemaphoreType.DMA((count,)),
            pltpu.SemaphoreType.DMA((count,)),
        ],
        compiler_params=pltpu.CompilerParams(collective_id=1, has_side_effects=True),
        name="give_back",
    )(parts, site_row, select)
    return (out[3], out[:3])


def solution(mesh):
    sizes = tuple(mesh.shape[a] for a in AXES)
    return jax.shard_map(
        functools.partial(shards, sizes),
        mesh=mesh,
        in_specs=(
            P(None, AXES),
            P(None, AXES),
            P(AXES),
            P(AXES),
            P(None, AXES),
            P(None, AXES),
            P(AXES),
            P(),
            P(),
            P(),
            P(),
            P(),
            P(),
            P(),
            P(),
        ),
        out_specs=(P(AXES), P(None, AXES)),
        check_vma=False,
    )
```

profile of v0, /device:TPU:1, one launch (start us, length us, event | category | flops | bytes accessed | tf_op | source)
XLA Modules:
  0.0 69.2 jit_solution(3723551538371231456)
XLA Ops:
  0.6 0.8 %copy.18.out_w_ref = f32[128,64]{1,0:T(8,128)S(1)} copy(f32[128,64]{0,1:T(8,128)} %param.27) | data formatting | bytes 65536 | tf_op args[11]
  1.5 0.0 copy-start.1
  1.5 0.9 %copy-done.1 = f32[384,128]{1,0:T(8,128)S(1)} copy-done((f32[384,128]{1,0:T(8,128)S(1)}, f32[384,128]{1,0:T(8,128)}, u32[]{:S(2)}) %copy-start.1) | copy-done | bytes 196632
  2.4 0.8 %copy-done.4 = f32[128,128]{1,0:T(8,128)S(1)} copy-done((f32[128,128]{1,0:T(8,128)S(1)}, f32[128,128]{1,0:T(8,128)}, u32[]{:S(2)}) %copy-start.4) | copy-done | bytes 65560
  3.3 0.8 %copy-done.5 = f32[128,128]{1,0:T(8,128)S(1)} copy-done((f32[128,128]{1,0:T(8,128)S(1)}, f32[128,128]{1,0:T(8,128)}, u32[]{:S(2)}) %copy-start.5) | copy-done | bytes 65560
  4.1 0.7 copy-done.9
  4.8 0.7 copy-done.10
  5.4 0.7 copy-done.11
  6.1 0.7 copy-done.12
  6.7 0.7 copy-done.13
  7.4 0.7 copy-done.14
  8.1 11.1 %ghosts.1 = (f32[136,128]{1,0:T(8,128)S(1)}, bf16[160,512]{1,0:T(8,128)(2,1)S(1)}) custom-call(f32[4]{0:T(128)S(1)} %copy-done.11, f32[4]{0:T(128)S(1)} %copy-done.12, f32[3,128]{1,0:T(4,128)S(1)} %copy-done.10, f32[128,128]{1,0:T(8,128)S(1)} %copy-done.4, s32[1,128]{1,0:T(1,128)S(1)} %bitcast.8, s32[1,128]{1,0:T(1,128)S(1)} %bitcast.9, ...), custom_call_target="tpu_custom_call" | custom-call | tf_op jit(solution)/shard_map/ghosts/pallas_call | solution.py:501
  19.2 2.2 %copy-done = bf16[16,512,256]{2,1,0:T(8,128)(2,1)S(1)} copy-done((bf16[16,512,256]{2,1,0:T(8,128)(2,1)S(1)}, bf16[16,512,256]{2,1,0:T(8,128)(2,1)}, u32[]{:S(2)}) %copy-start) | copy-done | bytes 4194328
  21.4 0.9 %copy-done.2 = f32[256,128]{1,0:T(8,128)S(1)} copy-done((f32[256,128]{1,0:T(8,128)S(1)}, f32[256,128]{1,0:T(8,128)}, u32[]{:S(2)}) %copy-start.2) | copy-done | bytes 131096
  22.3 0.8 %copy-done.6 = f32[3,32,128]{2,1,0:T(8,128)S(1)} copy-done((f32[3,32,128]{2,1,0:T(8,128)S(1)}, f32[3,32,128]{2,1,0:T(8,128)}, u32[]{:S(2)}) %copy-start.6) | copy-done | bytes 49176
  23.1 0.8 %copy-done.7 = f32[64,128]{1,0:T(8,128)S(1)} copy-done((f32[64,128]{1,0:T(8,128)S(1)}, f32[64,128]{1,0:T(8,128)}, u32[]{:S(2)}) %copy-start.7) | copy-done | bytes 32792
  23.9 0.7 copy-done.8
  24.6 0.7 copy-done.15
  25.2 31.1 %model.1.part_ref = f32[4,8,128]{2,1,0:T(8,128)S(1)} custom-call(f32[136,128]{1,0:T(8,128)S(1)} %get-tuple-element.4.own_ref, bf16[160,512]{1,0:T(8,128)(2,1)S(1)} %get-tuple-element.5.table_ref, bf16[16,512,256]{2,1,0:T(8,128)(2,1)S(1)} %copy-done, f32[3,32,128]{2,1,0:T(8,128)S(1)} %copy-done.6, f32[8,64]{1,0:T(8,128)S(1)} %copy-done.8, ...), custom_call_target="tpu_custom_call" | custom-call | tf_op jit(solution)/shard_map/model/pallas_call | solution.py:531
  56.3 0.0 copy-start.3
  56.3 0.6 copy-done.3
  56.9 9.9 %give_back.1 = f32[8,128]{1,0:T(8,128)} custom-call(f32[4,8,128]{2,1,0:T(8,128)} %copy-done.3, s32[1,128]{1,0:T(1,128)} %bitcast.6, f32[384,128]{1,0:T(8,128)} %constant.6.clone.select_ref), custom_call_target="tpu_custom_call" | custom-call | tf_op jit(solution)/shard_map/give_back/pallas_call | solution.py:571
  66.8 1.2 %slice_bitcast_fusion = f32[128]{0:T(128)} fusion(f32[8,128]{1,0:T(8,128)} %give_back.1), kind=kLoop, calls=%fused_computation | loop fusion | bytes 1024 | tf_op jit(solution)/shard_map/squeeze | solution.py:584
  68.0 1.3 %slice.7 = f32[3,128]{1,0:T(4,128)} slice(f32[8,128]{1,0:T(8,128)} %give_back.1), slice={[0:3], [0:128]} | slice | bytes 3072 | tf_op jit(solution)/shard_map/slice | solution.py:584
  (14 shorter events, 0.0 us)
Async XLA Ops:
  1.5 0.9 %copy-start.1 = (f32[384,128]{1,0:T(8,128)S(1)}, f32[384,128]{1,0:T(8,128)}, u32[]{:S(2)}) copy-start(f32[384,128]{1,0:T(8,128)} %constant.6.clone.select_ref) | copy-start | bytes 589828
  2.4 0.8 %copy-start.4 = (f32[128,128]{1,0:T(8,128)S(1)}, f32[128,128]{1,0:T(8,128)}, u32[]{:S(2)}) copy-start(f32[128,128]{1,0:T(8,128)} %attr_ref.1) | copy-start | bytes 196612
  3.3 0.8 %copy-start.5 = (f32[128,128]{1,0:T(8,128)S(1)}, f32[128,128]{1,0:T(8,128)}, u32[]{:S(2)}) copy-start(f32[128,128]{1,0:T(8,128)} %node_ref.1) | copy-start | bytes 196612
  4.1 0.7 copy-start.9
  4.8 0.7 copy-start.10
  5.4 0.7 copy-start.11
  6.1 0.7 copy-start.12
  6.7 0.7 copy-start.13
  7.4 0.7 copy-start.14
  19.2 2.2 %copy-start = (bf16[16,512,256]{2,1,0:T(8,128)(2,1)S(1)}, bf16[16,512,256]{2,1,0:T(8,128)(2,1)}, u32[]{:S(2)}) copy-start(bf16[16,512,256]{2,1,0:T(8,128)(2,1)} %constant.7.clone.hot_ref) | copy-start | bytes 12582916
  21.4 0.9 %copy-start.2 = (f32[256,128]{1,0:T(8,128)S(1)}, f32[256,128]{1,0:T(8,128)}, u32[]{:S(2)}) copy-start(f32[256,128]{1,0:T(8,128)} %in_ref.1) | copy-start | bytes 393220
  22.3 0.8 %copy-start.6 = (f32[3,32,128]{2,1,0:T(8,128)S(1)}, f32[3,32,128]{2,1,0:T(8,128)}, u32[]{:S(2)}) copy-start(f32[3,32,128]{2,1,0:T(8,128)} %constant.8.clone.shift_ref) | copy-start | bytes 147460
  23.1 0.8 %copy-start.7 = (f32[64,128]{1,0:T(8,128)S(1)}, f32[64,128]{1,0:T(8,128)}, u32[]{:S(2)}) copy-start(f32[64,128]{1,0:T(8,128)} %mix_ref.1) | copy-start | bytes 98308
  23.9 0.7 copy-start.8
  24.6 0.7 copy-start.15
  56.3 0.6 copy-start.3
where the time goes:
time: 70.4 us; the launch traced here: 69.2 us
  Pallas kernels  52.1 us (74%)
  local copies, waits for them, and re-layouts  16.5 us (23%)
    pallas_call x1, Pallas kernels, shards(): pl.pallas_call(functools.partial(model_kernel, slots, ch), out_shape=jax....  31.1 us
    unnamed x33, local copies, waits for them, and re-layouts  14 us
    pallas_call x1, Pallas kernels, shards(): pl.pallas_call(functools.partial(ghosts_kernel, groups, sizes, rows), out...  11.1 us
    pallas_call x1, Pallas kernels, shards(): pl.pallas_call(functools.partial(return_kernel, groups, sizes), out_shape...  9.86 us

commit v1 on v0

--- a/solution.py
+++ b/solution.py
@@ -11,6 +11,7 @@
 
 LXY = 8
 LZ = 2
+GROUP = 4
 SITES = LXY * LXY * LZ
 SPACING = 1.5
 CUTOFF = 4.0
@@ -23,7 +24,7 @@
 BF16 = jnp.bfloat16
 NT = (((1,), (1,)), ((), ()))
 VMEM = pl.BlockSpec(memory_space=pltpu.VMEM)
-SMEM = pl.BlockSpec(memory_space=pltpu.SMEM)
+ANY = pl.BlockSpec(memory_space=pl.ANY)
 
 
 def offsets():
@@ -99,9 +100,8 @@
                         start, sites = groups[key]
                         g = start + sites.index(inside)
                     hot[k, g, s] = 1.0
-    count = len(ds) // 2
-    hot = np.concatenate([hot[0::2], hot[1::2]], axis=2)
-    assert hot.shape == (count, rows, 2 * SITES)
+    hot = hot.reshape(len(ds) // GROUP, GROUP, rows, SITES).transpose(0, 2, 1, 3)
+    hot = hot.reshape(len(ds) // GROUP, rows, GROUP * SITES)
     return groups, select, hot, shift
 
 
@@ -149,32 +149,62 @@
     return jnp.where(slot == row, 1.0, 0.0).astype(F32)
 
 
-def ghosts_kernel(
-    groups, sizes, rows, scale_ref, shift_ref, pos_ref, attr_ref, species_ref, occ_ref, slots_ref,
-    node_ref, select_ref, own_ref, table_ref, send_buf, recv_buf, send_sem, recv_sem,
-):
+def thirds(x, axis):
+    first = x.astype(BF16).astype(F32)
+    rest = x - first
+    second = rest.astype(BF16).astype(F32)
+    return jnp.concatenate([first, second, rest - second], axis=axis).astype(BF16)
+
+
+def lanes_of(j):
+    return slice(j * SITES, (j + 1) * SITES)
+
+
+def sigmoid(v):
+    return 0.5 * jnp.tanh(0.5 * v) + 0.5
+
+
+def brick_kernel(groups, sizes, rows, slots, ch, names, *refs):
+    count = len(names)
+    hbm = dict(zip(names, refs[:count]))
+    energy_ref, force_ref = refs[count : count + 2]
+    local = dict(zip(names, refs[count + 2 : 2 * count + 2]))
+    (
+        load_sem, send_buf, recv_buf, send_sem, recv_sem, part_s, back_buf, back_send, back_recv,
+        table_ref, near_s, q_s, basis_s, y_s, env_s, first_s, sig_s, gain_s, raw_s, s_s,
+        ds_s, dt_s, dfirst_s, dgain_s, scal_s, dbasis_s, dy_s, g_s, lin_s, linb_s,
+    ) = refs[2 * count + 2 :]
+    loads = {
+        name: pltpu.make_async_copy(hbm[name], local[name], load_sem.at[n])
+        for n, name in enumerate(names)
+    }
+    for load in loads.values():
+        load.start()
     used = max(start + -(-len(sites) // 8) * 8 for start, sites in groups.values())
     if used < rows:
         recv_buf[used - SITES :, :] = jnp.zeros((rows - used, SITES), F32)
     barrier = greet(groups, sizes)
-    terms = exact(node_ref[...].T, attr_ref[...])
-    occ = occ_ref[...].astype(F32)
-    species = species_ref[...]
+    early = ("node", "attr", "pos", "occ", "species", "scale", "shift", "slots", "select")
+    for name in early:
+        loads[name].wait()
+
+    terms = dot(stack_lhs(local["node"][...].T), stack_rhs(local["attr"][...]))
+    occ = local["occ"][...].astype(F32)
+    species = local["species"][...]
     scale = jnp.zeros_like(occ)
     shift = jnp.zeros_like(occ)
-    for n in range(scale_ref.shape[0]):
-        scale = jnp.where(species == n, scale_ref[n], scale)
-        shift = jnp.where(species == n, shift_ref[n], shift)
+    for n in range(hbm["scale"].shape[1]):
+        scale = jnp.where(species == n, local["scale"][:, n : n + 1], scale)
+        shift = jnp.where(species == n, local["shift"][:, n : n + 1], shift)
     extra = jnp.concatenate(
-        [pos_ref[...], occ, occ * scale, occ * shift, jnp.zeros((2, SITES), F32)], axis=0
+        [local["pos"][...], occ, occ * scale, occ * shift, jnp.zeros((2, SITES), F32)], axis=0
     )
     data = jnp.concatenate([terms, extra], axis=0)
-    data = exact(data, slot_site(slots_ref[...]))
-    ch = terms.shape[0] // 2
-    own_ref[...] = data
+    hot_sites = slot_site(local["slots"][...]).astype(BF16)
+    data = dot(thirds(data, 1), jnp.concatenate([hot_sites] * 3, axis=0))
     sent = jnp.concatenate([data[ch:], jnp.zeros((SITES - ch - 8, SITES), F32)], axis=0)
-    wide = exact(select_ref[...], sent.T)
-    send_buf[...] = wide
+    select = local["select"][...]
+    send_buf[...] = dot(jnp.concatenate([select] * 3, axis=1), thirds(sent.T, 0))
     pl.semaphore_wait(barrier, len(groups))
     copies = []
     for n, (o, (start, sites)) in enumerate(groups.items()):
@@ -192,49 +222,67 @@
         )
     for copy in copies:
         copy.start()
-    for copy in copies:
-        copy.wait()
-
-    for t in range(rows // SITES):
-        if t == 0:
-            near, q = data[ch : 2 * ch], data[2 * ch :]
-        else:
-            block = recv_buf[(t - 1) * SITES : t * SITES, :].T
-            near, q = block[:ch], block[ch : ch + 8]
+
+    for name in names:
+        if name not in early:
+            loads[name].wait()
+    radial = local["radial"][...]
+    mix = local["mix"][...]
+    mix3_t = stack_lhs(mix.T)
+    mix3 = stack_lhs(mix)
+    lin_s[...] = stack_lhs(local["latent_in"][...].T)
+    linb_s[...] = stack_lhs(local["latent_in"][...])
+    basis_n = radial.shape[0]
+    radial_high = radial.astype(BF16).astype(F32)
+    radial_t = jnp.concatenate(
+        [radial_high, radial_high, radial - radial_high, jnp.zeros_like(radial)], axis=0
+    ).T.astype(BF16)
+    radial3 = stack_lhs(jnp.concatenate([radial, jnp.zeros_like(radial)], axis=0))
+    readout_row = local["readout"][...]
+
+    def eye(n):
+        return lax.broadcasted_iota(jnp.int32, (n, n), 0) == lax.broadcasted_iota(
+            jnp.int32, (n, n), 1
+        )
+
+    r_col = jnp.sum(jnp.where(eye(ch), readout_row, 0.0), axis=1, keepdims=True)
+    v_row = jnp.sum(local["latent_out"][...] * r_col, axis=0, keepdims=True)
+    v_col = jnp.sum(jnp.where(eye(v_row.shape[1]), v_row, 0.0), axis=1, keepdims=True)
+    shift_ref = local["images"]
+    hot_ref = local["hot"]
+
+    def fill(t, near, q):
         near_high = near.astype(BF16).astype(F32)
         q1 = q.astype(BF16).astype(F32)
         q2 = (q - q1).astype(BF16).astype(F32)
-        table_ref[:, t * SITES : (t + 1) * SITES] = jnp.concatenate(
+        table_ref[:, lanes_of(t)] = jnp.concatenate(
             [near_high, near - near_high, q1, q2, q - q1 - q2, jnp.zeros_like(q)], axis=0
         ).astype(BF16)
 
-
-def sigmoid(v):
-    return 1.0 / (1.0 + jnp.exp(-v))
-
-
-def model_kernel(
-    slots, ch, own_ref, table_ref, hot_ref, shift_ref, radial_ref, mix_ref, in_ref, out_w_ref,
-    readout_ref, result_ref, near_s, q_s, basis_s, y_s, env_s, first_s, sig_s, gain_s, raw_s, s_s,
-    ds_s, dt_s, dfirst_s, dgain_s, scal_s, dbasis_s, dy_s, g_s, lin_s, linb_s,
-):
-    pairs = slots // 2
+    fill(0, data[ch : 2 * ch], data[2 * ch :])
+    for copy in copies:
+        copy.wait()
+    for t in range(1, rows // SITES):
+        block = recv_buf[(t - 1) * SITES : t * SITES, :].T
+        fill(t, block[:ch], block[ch : ch + 8])
+
+    steps = slots // GROUP
     inv_root = 1.0 / math.sqrt(slots)
     table = table_ref[...]
 
     def fetch(p, carry):
         got = dot(table, hot_ref[p])
-        for j in range(2):
-            k = 2 * p + j
-            part = got[:, j * SITES : (j + 1) * SITES]
+        for j in range(GROUP):
+            k = GROUP * p + j
+            part = got[:, lanes_of(j)]
             near_s[k] = part[:ch] + part[ch : 2 * ch]
             q = 2 * ch
             q_s[k] = part[q : q + 8] + part[q + 8 : q + 16] + part[q + 16 : q + 24]
         return carry
 
-    lax.fori_loop(0, pairs, fetch, 0)
-
-    extra = own_ref[2 * ch : 2 * ch + 8]
+    lax.fori_loop(0, steps, fetch, 0)
+
+    extra = data[2 * ch :]
     ebar = extra[4:5]
     rx = (q_s[:, 0, :] + shift_ref[0]) - extra[0:1]
     ry = (q_s[:, 1, :] + shift_ref[1]) - extra[1:2]
@@ -259,37 +307,37 @@
     angle = d * (math.pi / CUTOFF)
     sines = [jnp.sin(angle)]
     cosines = [jnp.cos(angle)]
-    for n in range(1, radial_ref.shape[0]):
+    for n in range(1, basis_n):
         sines.append(sines[0] * cosines[-1] + cosines[0] * sines[-1])
         cosines.append(cosines[0] * cosines[-1] - sines[0] * sines[n - 1])
-    for n in range(radial_ref.shape[0]):
+    for n in range(basis_n):
         basis_s[:, n, :] = sines[n] * inv
 
-    centre = own_ref[:ch]
-    radial_t = radial_ref[...].T
-    mix3_t = stack_lhs(mix_ref[...].T)
+    centre = data[:ch]
 
     def first(p, carry):
-        basis = jnp.concatenate([basis_s[2 * p], basis_s[2 * p + 1]], axis=1)
-        radial = exact(radial_t, basis)
+        basis = jnp.concatenate([basis_s[GROUP * p + j] for j in range(GROUP)], axis=1)
+        high = basis.astype(BF16).astype(F32)
+        basis = jnp.concatenate([high, basis - high, high, jnp.zeros_like(high)], axis=0)
+        radial = dot(radial_t, basis.astype(BF16))
         total = []
-        for j in range(2):
-            k = 2 * p + j
-            v = radial[:, j * SITES : (j + 1) * SITES] + centre + near_s[k]
+        for j in range(GROUP):
+            k = GROUP * p + j
+            v = radial[:, lanes_of(j)] + centre + near_s[k]
             sig = sigmoid(v)
             act = v * sig
             first_s[k] = act
             sig_s[k] = sig * (1.0 + v * (1.0 - sig))
             total.append(act)
         mixture = dot(mix3_t, stack_rhs(jnp.concatenate(total, axis=1)))
-        for j in range(2):
-            k = 2 * p + j
-            part = mixture[:, j * SITES : (j + 1) * SITES]
+        for j in range(GROUP):
+            k = GROUP * p + j
+            part = mixture[:, lanes_of(j)]
             gain_s[k] = part[:ch]
             raw_s[k] = part[ch:]
         return carry
 
-    lax.fori_loop(0, pairs, first, 0)
+    lax.fori_loop(0, steps, first, 0)
 
     step = 16
     for c in range(0, ch, step):
@@ -304,17 +352,10 @@
         for m in range(9):
             s_s[m, c : c + step, :] = acc[m] * inv_root
 
-    lin_s[...] = stack_lhs(in_ref[...].T)
-    linb_s[...] = stack_lhs(in_ref[...])
-    readout_row = readout_ref[...]
-    v_col = jnp.sum(out_w_ref[...] * readout_row, axis=1, keepdims=True)
-    same = lax.broadcasted_iota(jnp.int32, (ch, ch), 0) == lax.broadcasted_iota(jnp.int32, (ch, ch), 1)
-    r_col = jnp.sum(jnp.where(same, readout_row, 0.0), axis=1, keepdims=True)
-
     def middle(p, energy):
         feats, gains, t1s, t2s, envs = [], [], [], [], []
-        for j in range(2):
-            k = 2 * p + j
+        for j in range(GROUP):
+            k = GROUP * p + j
             y = [y_s[k, m : m + 1, :] for m in range(9)]
             t1 = y[1] * s_s[1]
             for m in (2, 3):
@@ -336,9 +377,9 @@
         dhidden = slope * (v_col * weight)
         dfeat = dot(linb_s[...], stack_rhs(dhidden))
         ract = jnp.sum(v_col * act, axis=0, keepdims=True)
-        for j in range(2):
-            k = 2 * p + j
-            lanes = slice(j * SITES, (j + 1) * SITES)
+        for j in range(GROUP):
+            k = GROUP * p + j
+            lanes = lanes_of(j)
             raw = ract[:, lanes] + jnp.sum(r_col * feats[j][:ch], axis=0, keepdims=True)
             scal_s[pl.ds(k, 1), :] = raw
             energy = energy + raw * envs[j]
@@ -349,7 +390,7 @@
             dt_s[k] = jnp.concatenate([gains[j] * d0, gains[j] * d1, gains[j] * d2], axis=0)
         return energy
 
-    energy = lax.fori_loop(0, pairs, middle, jnp.zeros((1, SITES), F32))
+    energy = lax.fori_loop(0, steps, middle, jnp.zeros((1, SITES), F32))
 
     for c in range(0, ch, step):
 
@@ -366,13 +407,10 @@
         for m in range(9):
             ds_s[m, c : c + step, :] = acc[m] * inv_root
 
-    mix3 = stack_lhs(mix_ref[...])
-    radial3 = stack_lhs(jnp.concatenate([radial_ref[...], jnp.zeros((8, ch), F32)], axis=0))
-
     def last(p, carry):
         dmix = []
-        for j in range(2):
-            k = 2 * p + j
+        for j in range(GROUP):
+            k = GROUP * p + j
             env = env_s[pl.ds(k, 1), :]
             raw = raw_s[k]
             w = raw * env
@@ -390,18 +428,18 @@
             dmix.append(jnp.concatenate([dgain_s[k], dw * env], axis=0))
         dfirst = dot(mix3, stack_rhs(jnp.concatenate(dmix, axis=1)))
         dsum = []
-        for j in range(2):
-            k = 2 * p + j
-            dsum.append((dfirst[:, j * SITES : (j + 1) * SITES] + dfirst_s[k]) * sig_s[k])
+        for j in range(GROUP):
+            k = GROUP * p + j
+            dsum.append((dfirst[:, lanes_of(j)] + dfirst_s[k]) * sig_s[k])
         dbasis = dot(radial3, stack_rhs(jnp.concatenate(dsum, axis=1)))
-        for j in range(2):
-            dbasis_s[2 * p + j] = dbasis[:8, j * SITES : (j + 1) * SITES]
+        for j in range(GROUP):
+            dbasis_s[GROUP * p + j] = dbasis[:8, lanes_of(j)]
         return carry
 
-    lax.fori_loop(0, pairs, last, 0)
+    lax.fori_loop(0, steps, last, 0)
 
     dd = scal_s[...] * denv_dd
-    for n in range(radial_ref.shape[0]):
+    for n in range(basis_n):
         rate = (n + 1) * math.pi / CUTOFF
         dd = dd + dbasis_s[:, n, :] * ((rate * cosines[n] - sines[n] * inv) * inv)
     y1, y2, y3, y4, y5, y6, y7, y8 = [dy_s[:, m, :] for m in range(1, 9)]
@@ -422,32 +460,24 @@
         g_s[:, 8 + n, :] = zero
 
     def spread(p, acc):
-        g = jnp.concatenate([g_s[2 * p], g_s[2 * p + 1]], axis=1).astype(BF16)
+        g = jnp.concatenate([g_s[GROUP * p + j] for j in range(GROUP)], axis=1).astype(BF16)
         return acc + lax.dot_general(g, hot_ref[p], NT, preferred_element_type=F32)
 
-    rows = table_ref.shape[1]
-    acc = lax.fori_loop(0, pairs, spread, jnp.zeros((16, rows), F32))
+    acc = lax.fori_loop(0, steps, spread, jnp.zeros((16, rows), F32))
     acc = -(acc[:8] + acc[8:])
     own.append(ebar * energy + extra[5:6])
     own.append(jnp.zeros((4, SITES), F32))
-    result_ref[0] = acc[:, :SITES] + jnp.concatenate(own, axis=0)
+    part_s[0] = acc[:, :SITES] + jnp.concatenate(own, axis=0)
     for t in range(1, rows // SITES):
-        result_ref[t] = acc[:, t * SITES : (t + 1) * SITES]
-
-
-def return_kernel(
-    groups, sizes, part_ref, slots_ref, select_ref, out_ref, recv_buf, send_sem, recv_sem
-):
-    barrier = greet(groups, sizes)
-    pl.semaphore_wait(barrier, len(groups))
+        part_s[t] = acc[:, lanes_of(t)]
     copies = []
     for n, (o, (start, _)) in enumerate(groups.items()):
         copies.append(
             pltpu.make_async_remote_copy(
-                src_ref=part_ref.at[start // SITES],
-                dst_ref=recv_buf.at[n],
-                send_sem=send_sem.at[n],
-                recv_sem=recv_sem.at[n],
+                src_ref=part_s.at[start // SITES],
+                dst_ref=back_buf.at[n],
+                send_sem=back_send.at[n],
+                recv_sem=back_recv.at[n],
                 device_id=device_at(o, sizes),
                 device_id_type=pl.DeviceIdType.MESH,
             )
@@ -457,18 +487,17 @@
     for copy in copies:
         copy.wait()
     lane = lax.broadcasted_iota(jnp.int32, (8, SITES), 1)
-    total = part_ref[0]
-    merged = [jnp.zeros((8, SITES), F32) for _ in range(part_ref.shape[0])]
+    merged = [jnp.zeros((8, SITES), F32) for _ in range(rows // SITES)]
     for n, (start, sites) in enumerate(groups.values()):
         t, low = start // SITES, start % SITES
         live = (lane >= low) & (lane < low + len(sites))
-        merged[t] = merged[t] + jnp.where(live, recv_buf[n], 0.0)
-    total = total + exact(
-        jnp.concatenate(merged[1:], axis=1), select_ref[...]
-    )
-    out_ref[...] = lax.dot_general(
-        total, slot_site(slots_ref[...]), NT, precision=PRECISE, preferred_element_type=F32
-    )
+        merged[t] = merged[t] + jnp.where(live, back_buf[n], 0.0)
+    select3 = jnp.concatenate([local["select"][...]] * 3, axis=0)
+    total = part_s[0] + dot(thirds(jnp.concatenate(merged[1:], axis=1), 1), select3)
+    hot3 = jnp.concatenate([slot_site(local["slots"][...]).astype(BF16)] * 3, axis=1)
+    out = lax.dot_general(thirds(total, 1), hot3, NT, preferred_element_type=F32)
+    energy_ref[...] = out[3:4]
+    force_ref[...] = out[:3]
 
 
 def shards(
@@ -489,51 +518,53 @@
     species_scale,
     species_shift,
 ):
-    groups, select, hot, shift = lattice_plan(sizes[2])
+    groups, select, hot, images = lattice_plan(sizes[2])
     rows = hot.shape[1]
-    slots = shift.shape[1]
+    slots = images.shape[1]
     ch = mix_weight.shape[0]
     hid = latent_in.shape[1]
     count = len(groups)
-    select = jnp.asarray(select[SITES:])
-    hot = jnp.asarray(hot, dtype=BF16)
-    site_row = site_slots.reshape(1, SITES)
-    own, table = pl.pallas_call(
-        functools.partial(ghosts_kernel, groups, sizes, rows),
+    operands = {
+        "node": node_weight,
+        "attr": attributes,
+        "pos": positions,
+        "occ": occupied.reshape(1, SITES),
+        "species": species.reshape(1, SITES),
+        "scale": species_scale.reshape(1, -1),
+        "shift": species_shift.reshape(1, -1),
+        "slots": site_slots.reshape(1, SITES),
+        "select": jnp.asarray(select[SITES:], dtype=BF16),
+        "hot": jnp.asarray(hot, dtype=BF16),
+        "images": jnp.asarray(images),
+        "radial": radial_weight,
+        "mix": mix_weight,
+        "latent_in": latent_in,
+        "latent_out": latent_out.T,
+        "readout": readout.reshape(1, ch),
+    }
+    names = tuple(operands)
+    dma = pltpu.SemaphoreType.DMA
+    per_slot = lambda *dims: pltpu.VMEM((slots,) + dims + (SITES,), F32)
+    energy, forces = pl.pallas_call(
+        functools.partial(brick_kernel, groups, sizes, rows, slots, ch, names),
         out_shape=(
-            jax.ShapeDtypeStruct((2 * ch + 8, SITES), F32),
-            jax.ShapeDtypeStruct((2 * ch + 32, rows), BF16),
+            jax.ShapeDtypeStruct((1, SITES), F32),
+            jax.ShapeDtypeStruct((3, SITES), F32),
         ),
-        in_specs=[SMEM] * 2 + [VMEM] * 7,
+        in_specs=[ANY] * len(names),
         out_specs=(VMEM, VMEM),
-        scratch_shapes=[
+        scratch_shapes=[pltpu.VMEM(v.shape, v.dtype) for v in operands.values()]
+        + [
+            dma((len(names),)),
             pltpu.VMEM((rows - SITES, SITES), F32),
             pltpu.VMEM((rows - SITES, SITES), F32),
-            pltpu.SemaphoreType.DMA((count,)),
-            pltpu.SemaphoreType.DMA((count,)),
-        ],
-        compiler_params=pltpu.CompilerParams(
-            collective_id=0, has_side_effects=True, vmem_limit_bytes=16 * 2**20
-        ),
-        name="ghosts",
-    )(
-        species_scale,
-        species_shift,
-        positions,
-        attributes,
-        species.reshape(1, SITES),
-        occupied.reshape(1, SITES),
-        site_row,
-        node_weight,
-        select,
-    )
-    per_slot = lambda *dims: pltpu.VMEM((slots,) + dims + (SITES,), F32)
-    parts = pl.pallas_call(
-        functools.partial(model_kernel, slots, ch),
-        out_shape=jax.ShapeDtypeStruct((rows // SITES, 8, SITES), F32),
-        in_specs=[VMEM] * 9,
-        out_specs=VMEM,
-        scratch_shapes=[
+            dma((count,)),
+            dma((count,)),
+            pltpu.VMEM((rows // SITES, 8, SITES), F32),
+            pltpu.VMEM((count, 8, SITES), F32),
+            dma((count,)),
+            dma((count,)),
+            pltpu.VMEM((2 * ch + 32, rows), BF16),
             per_slot(ch),
             per_slot(8),
             per_slot(8),
@@ -555,33 +586,12 @@
             pltpu.VMEM((hid, 12 * ch), BF16),
             pltpu.VMEM((4 * ch, 3 * hid), BF16),
         ],
-        compiler_params=pltpu.CompilerParams(vmem_limit_bytes=40 * 2**20),
-        name="model",
-    )(
-        own,
-        table,
-        hot,
-        jnp.asarray(shift),
-        radial_weight,
-        mix_weight,
-        latent_in,
-        latent_out,
-        readout.reshape(1, ch),
-    )
-    out = pl.pallas_call(
-        functools.partial(return_kernel, groups, sizes),
-        out_shape=jax.ShapeDtypeStruct((8, SITES), F32),
-        in_specs=[VMEM] * 3,
-        out_specs=VMEM,
-        scratch_shapes=[
-            pltpu.VMEM((count, 8, SITES), F32),
-            pltpu.SemaphoreType.DMA((count,)),
-            pltpu.SemaphoreType.DMA((count,)),
-        ],
-        compiler_params=pltpu.CompilerParams(collective_id=1, has_side_effects=True),
-        name="give_back",
-    )(parts, site_row, select)
-    return (out[3], out[:3])
+        compiler_params=pltpu.CompilerParams(
+            collective_id=0, has_side_effects=True, vmem_limit_bytes=56 * 2**20
+        ),
+        name="brick",
+    )(*operands.values())
+    return (energy.reshape(SITES), forces)
 
 
 def solution(mesh):

time: 70.4 us -> 41.9 us (0.60); the launches traced: 69.2 us -> 41.7 us
  local copies, waits for them, and re-layouts: 16.5 us -> 2.39 us
  Pallas kernels: 52.1 us -> 38.7 us
    pallas_call x3 -> x1, Pallas kernels: 52.1 us -> 38.7 us  [shards(): pl.pallas_call(functools.partial(brick_kernel, groups, sizes, rows, slots...]
    unnamed x33 -> x2, local copies, waits for them, and re-layouts: 14 us -> 2.39 us
    slice x1 -> x0, local copies, waits for them, and re-layouts: 1.26 us -> none  [shards(): return (out[3], out[:3])]
    squeeze x1 -> x0, local copies, waits for them, and re-layouts: 1.2 us -> none  [shards(): return (out[3], out[:3])]
where the time goes in v1:
time: 41.9 us; the launch traced here: 41.7 us
  Pallas kernels  38.7 us (92%)
  local copies, waits for them, and re-layouts  2.39 us (6%)
  between operations  0.64 us (2%)
    pallas_call x1, Pallas kernels, shards(): pl.pallas_call(functools.partial(brick_kernel, groups, sizes, rows, slots...  38.7 us
    unnamed x2, local copies, waits for them, and re-layouts  2.39 us

profile of v1, /device:TPU:1, one launch (start us, length us, event | category | flops | bytes accessed | tf_op | source)
XLA Modules:
  0.0 41.7 jit_solution(16236592967239488984)
XLA Ops:
  0.6 38.7 %brick.1 = (f32[1,128]{1,0:T(1,128)}, f32[3,128]{1,0:T(4,128)}) custom-call(f32[128,128]{1,0:T(8,128)} %refs_0_.1, f32[128,128]{1,0:T(8,128)} %refs_1_.1, f32[3,128]{1,0:T(4,128)} %refs_2_.1, s32[1,128]{1,0:T(1,128)} %bitcast.9, s32[1,128]{1,0:T(1,128)} %bitcast.10, f32[1,4]{1,0:T(1,128)} %bitcast.11, f32[1,4]{1,0:T(1,128)} %bitcast.12, s32[1,128]{1,0:T(1,128)} %bitcast.13, ...), custom_call_target="tpu_custom_call" | custom-call | tf_op jit(solution)/shard_map/brick/pallas_call | solution.py:548
  39.4 1.1 %copy.20 = f32[128]{0:T(128)} copy(f32[128]{0:T(128)} %bitcast.15) | data formatting | bytes 1024
  40.5 1.2 %copy.21 = f32[3,128]{1,0:T(4,128)} copy(f32[3,128]{1,0:T(4,128)} %get-tuple-element.9) | data formatting | bytes 3072

commit v2 on v1

--- a/solution.py
+++ b/solution.py
@@ -11,7 +11,7 @@
 
 LXY = 8
 LZ = 2
-GROUP = 4
+GROUP = 16
 SITES = LXY * LXY * LZ
 SPACING = 1.5
 CUTOFF = 4.0
@@ -105,6 +105,10 @@
     return groups, select, hot, shift
 
 
+def whole_face(o):
+    return o[:2] == (0, 0)
+
+
 def device_at(o, sizes):
     return tuple(
         lax.rem(lax.axis_index(a) + (c + n), n) if c else lax.axis_index(a)
@@ -170,7 +174,7 @@
     energy_ref, force_ref = refs[count : count + 2]
     local = dict(zip(names, refs[count + 2 : 2 * count + 2]))
     (
-        load_sem, send_buf, recv_buf, send_sem, recv_sem, part_s, back_buf, back_send, back_recv,
+        load_sem, face_out, face_in, send_buf, recv_buf, send_sem, recv_sem, part_s, back_buf, back_send, back_recv,
         table_ref, near_s, q_s, basis_s, y_s, env_s, first_s, sig_s, gain_s, raw_s, s_s,
         ds_s, dt_s, dfirst_s, dgain_s, scal_s, dbasis_s, dy_s, g_s, lin_s, linb_s,
     ) = refs[2 * count + 2 :]
@@ -202,18 +206,24 @@
     data = jnp.concatenate([terms, extra], axis=0)
     hot_sites = slot_site(local["slots"][...]).astype(BF16)
     data = dot(thirds(data, 1), jnp.concatenate([hot_sites] * 3, axis=0))
+    face_out[...] = data[ch:]
     sent = jnp.concatenate([data[ch:], jnp.zeros((SITES - ch - 8, SITES), F32)], axis=0)
     select = local["select"][...]
     send_buf[...] = dot(jnp.concatenate([select] * 3, axis=1), thirds(sent.T, 0))
     pl.semaphore_wait(barrier, len(groups))
     copies = []
-    for n, (o, (start, sites)) in enumerate(groups.items()):
+    face_tiles = []
+    for n, (o, (start, sites)) in enumerate(sorted(groups.items(), key=lambda v: not whole_face(v[0]))):
         back = tuple(-c for c in o)
         part = pl.ds(start - SITES, -(-len(sites) // 8) * 8)
+        source, target = send_buf.at[part], recv_buf.at[part]
+        if whole_face(o):
+            source, target = face_out, face_in.at[len(face_tiles)]
+            face_tiles.append(start // SITES)
         copies.append(
             pltpu.make_async_remote_copy(
-                src_ref=send_buf.at[part],
-                dst_ref=recv_buf.at[part],
+                src_ref=source,
+                dst_ref=target,
                 send_sem=send_sem.at[n],
                 recv_sem=recv_sem.at[n],
                 device_id=device_at(back, sizes),
@@ -263,7 +273,10 @@
     for copy in copies:
         copy.wait()
     for t in range(1, rows // SITES):
-        block = recv_buf[(t - 1) * SITES : t * SITES, :].T
+        if t in face_tiles:
+            block = face_in[face_tiles.index(t)]
+        else:
+            block = recv_buf[(t - 1) * SITES : t * SITES, :].T
         fill(t, block[:ch], block[ch : ch + 8])
 
     steps = slots // GROUP
@@ -459,17 +472,18 @@
         g_s[:, n, :] = zero
         g_s[:, 8 + n, :] = zero
 
-    def spread(p, acc):
-        g = jnp.concatenate([g_s[GROUP * p + j] for j in range(GROUP)], axis=1).astype(BF16)
-        return acc + lax.dot_general(g, hot_ref[p], NT, preferred_element_type=F32)
-
-    acc = lax.fori_loop(0, steps, spread, jnp.zeros((16, rows), F32))
-    acc = -(acc[:8] + acc[8:])
-    own.append(ebar * energy + extra[5:6])
-    own.append(jnp.zeros((4, SITES), F32))
-    part_s[0] = acc[:, :SITES] + jnp.concatenate(own, axis=0)
+    def spread(first_row, size):
+        def add(p, acc):
+            g = jnp.concatenate([g_s[GROUP * p + j] for j in range(GROUP)], axis=1).astype(BF16)
+            hot = hot_ref[p, first_row : first_row + size, :]
+            return acc + lax.dot_general(g, hot, NT, preferred_element_type=F32)
+
+        acc = lax.fori_loop(0, steps, add, jnp.zeros((16, size), F32), unroll=True)
+        return -(acc[:8] + acc[8:])
+
+    acc = spread(SITES, rows - SITES)
     for t in range(1, rows // SITES):
-        part_s[t] = acc[:, lanes_of(t)]
+        part_s[t] = acc[:, lanes_of(t - 1)]
     copies = []
     for n, (o, (start, _)) in enumerate(groups.items()):
         copies.append(
@@ -484,6 +498,9 @@
         )
     for copy in copies:
         copy.start()
+    own.append(ebar * energy + extra[5:6])
+    own.append(jnp.zeros((4, SITES), F32))
+    total = spread(0, SITES) + jnp.concatenate(own, axis=0)
     for copy in copies:
         copy.wait()
     lane = lax.broadcasted_iota(jnp.int32, (8, SITES), 1)
@@ -493,7 +510,7 @@
         live = (lane >= low) & (lane < low + len(sites))
         merged[t] = merged[t] + jnp.where(live, back_buf[n], 0.0)
     select3 = jnp.concatenate([local["select"][...]] * 3, axis=0)
-    total = part_s[0] + dot(thirds(jnp.concatenate(merged[1:], axis=1), 1), select3)
+    total = total + dot(thirds(jnp.concatenate(merged[1:], axis=1), 1), select3)
     hot3 = jnp.concatenate([slot_site(local["slots"][...]).astype(BF16)] * 3, axis=1)
     out = lax.dot_general(thirds(total, 1), hot3, NT, preferred_element_type=F32)
     energy_ref[...] = out[3:4]
@@ -524,6 +541,7 @@
     ch = mix_weight.shape[0]
     hid = latent_in.shape[1]
     count = len(groups)
+    faces = sum(whole_face(o) for o in groups)
     operands = {
         "node": node_weight,
         "attr": attributes,
@@ -556,6 +574,8 @@
         scratch_shapes=[pltpu.VMEM(v.shape, v.dtype) for v in operands.values()]
         + [
             dma((len(names),)),
+            pltpu.VMEM((ch + 8, SITES), F32),
+            pltpu.VMEM((faces, ch + 8, SITES), F32),
             pltpu.VMEM((rows - SITES, SITES), F32),
             pltpu.VMEM((rows - SITES, SITES), F32),
             dma((count,)),

time: 41.9 us -> 34.9 us (0.83)
  Pallas kernels: 38.7 us -> 31.7 us
    pallas_call x1, Pallas kernels: 38.7 us -> 31.7 us  [shards(): pl.pallas_call(functools.partial(brick_kernel, groups, sizes, rows, slots...]
where the time goes in v2:
time: 34.9 us; the launch traced here: 34.7 us
  Pallas kernels  31.7 us (91%)
  local copies, waits for them, and re-layouts  2.39 us (7%)
  between operations  0.64 us (2%)
    pallas_call x1, Pallas kernels, shards(): pl.pallas_call(functools.partial(brick_kernel, groups, sizes, rows, slots...  31.7 us
    unnamed x2, local copies, waits for them, and re-layouts  2.39 us

profile of v2, /device:TPU:1, one launch (start us, length us, event | category | flops | bytes accessed | tf_op | source)
XLA Modules:
  0.0 34.7 jit_solution(13070714558155979605)
XLA Ops:
  0.6 31.7 %brick.1 = (f32[1,128]{1,0:T(1,128)}, f32[3,128]{1,0:T(4,128)}) custom-call(f32[128,128]{1,0:T(8,128)} %refs_0_.1, f32[128,128]{1,0:T(8,128)} %refs_1_.1, f32[3,128]{1,0:T(4,128)} %refs_2_.1, s32[1,128]{1,0:T(1,128)} %bitcast.9, s32[1,128]{1,0:T(1,128)} %bitcast.10, f32[1,4]{1,0:T(1,128)} %bitcast.11, f32[1,4]{1,0:T(1,128)} %bitcast.12, s32[1,128]{1,0:T(1,128)} %bitcast.13, ...), custom_call_target="tpu_custom_call" | custom-call | tf_op jit(solution)/shard_map/brick/pallas_call | solution.py:566
  32.4 1.1 %copy.20 = f32[128]{0:T(128)} copy(f32[128]{0:T(128)} %bitcast.15) | data formatting | bytes 1024
  33.5 1.2 %copy.21 = f32[3,128]{1,0:T(4,128)} copy(f32[3,128]{1,0:T(4,128)} %get-tuple-element.9) | data formatting | bytes 3072
